TPU v7x, 32 devices: a whole 2x2x4 slice. The times are simulated.
32 devices in a mesh: slab: 8 (over y, x, core), field: 4 (over z).
Axes of the slice: x: 2, y: 2, z: 4, core: 2. Of those that a mesh axis runs over, the one named last changes fastest.
Arguments:
- snaps: bfloat16 [4, 16, 3, 32, 2048], P('field', 'slab'), may hold values from -6 to 6
- writer_map: int32 [64], replicated, may hold values from 0 to 63, each once
- omega: int32 [64, 64], replicated, may hold values from -3 to 3
- face_level: int32 [32], replicated, may hold values from 0 to 11
Outputs:
- sketch_rows: float32 [4, 16, 64], P('field')
- core: float32 [64, 64], replicated
All inputs are finite; a program needn't handle non-finite values.
Results may differ from a plain program's by a relative error of at most 0.00035.
Values may be sent and summed in bfloat16 or wider, within the bound.
A program may use at most 128 MiB of HBM per device.

v0:
```python
import jax
import jax.numpy as jnp
from jax import lax
from jax.sharding import PartitionSpec as P


def from_behind(block, axis, distance):
    devices = range(lax.axis_size(axis))
    route = [(i - distance, i) for i in devices if i - distance in devices]
    return lax.ppermute(block, axis, route)


def body(snaps, writer_map, omega, face_level):
    field_count = lax.axis_size("field")
    slab_at = lax.axis_index("slab")
    field_at = lax.axis_index("field")
    sketch_cols = omega.shape[1]
    total_snaps = omega.shape[0]
    total_planes = face_level.shape[0]
    group_rows = total_snaps // field_count
    columns = jnp.arange(total_snaps, dtype=jnp.int32)
    onehot = (writer_map[:, None] == columns[None, :]).astype(jnp.bfloat16)
    test_all = jnp.dot(
        onehot, omega.astype(jnp.bfloat16), preferred_element_type=jnp.float32
    ).astype(jnp.bfloat16)
    local = lax.all_to_all(snaps, "slab", split_axis=3, concat_axis=1, tiled=True)
    comps = local.shape[2]
    planes_dev = local.shape[3]
    cells = local.shape[4]
    features = comps * planes_dev * cells
    test_own = lax.dynamic_slice_in_dim(test_all, field_at * group_rows, group_rows, 0)
    flat = local.reshape(group_rows, features)
    partial_z = jnp.dot(test_own.T, flat, preferred_element_type=jnp.float32)
    sketched = lax.psum(partial_z.astype(jnp.bfloat16), "field").astype(jnp.float32)
    sketched = sketched.reshape(sketch_cols, comps, planes_dev, cells)
    spacing = 0.5 * jnp.power(jnp.float32(1.12), face_level.astype(jnp.float32))
    first_plane = slab_at * planes_dev
    weight = lax.dynamic_slice_in_dim(spacing, first_plane, planes_dev, 0).reshape(
        1, 1, planes_dev, 1
    )
    coupling = lax.dynamic_slice_in_dim(1.0 / spacing, first_plane, planes_dev, 0).reshape(
        1, 1, planes_dev, 1
    )
    scale = 1.0 / (comps * total_planes * cells)
    lower = from_behind(
        sketched[:, :, -1:].astype(jnp.bfloat16), ("slab", "field"), field_count
    ).astype(jnp.float32)
    below = jnp.concatenate([lower, sketched[:, :, :-1]], axis=2)
    flux = coupling * (sketched - below)
    upper = from_behind(
        flux[:, :, :1].astype(jnp.bfloat16), ("slab", "field"), -field_count
    ).astype(jnp.float32)
    above = jnp.concatenate([flux[:, :, 1:], upper], axis=2)
    applied = (
        ((weight * sketched + flux - above) * scale)
        .astype(jnp.bfloat16)
        .reshape(sketch_cols, features)
    )
    partial_rows = lax.dot_general(
        flat, applied, (((1,), (1,)), ((), ())), preferred_element_type=jnp.float32
    )
    blocks = (jnp.arange(field_count, dtype=jnp.int32) == field_at).astype(jnp.float32)
    stored_rows = (blocks[:, None, None] * partial_rows[None, :, :]).reshape(
        total_snaps, sketch_cols
    )
    rows = lax.psum(stored_rows, ("slab", "field"))
    core = (
        jnp.dot(test_all.astype(jnp.float32).T, rows, precision=lax.Precision.HIGHEST) / total_snaps
    )
    own_rows = lax.dynamic_slice_in_dim(rows, field_at * group_rows, group_rows, 0)
    return (own_rows.reshape(1, group_rows, sketch_cols), core)


def solution(mesh):
    in_specs = (P("field", "slab", None, None, None), P(), P(), P())
    out_specs = (P("field", None, None), P())
    return jax.shard_map(body, mesh=mesh, in_specs=in_specs, out_specs=out_specs, check_vma=False)
```

profile of v0, /device:TPU:0, one launch (start us, length us, event | category | flops | bytes accessed | tf_op | source)
XLA Modules:
  0.0 285.8 jit_solution(11686878091657337957)
XLA Ops:
  7.2 2.8 copy.7
  10.0 5.2 %all-to-all-start = ((bf16[1,2,3,32,2048]{4,2,1,0,3:T(4,128)(2,1)}), bf16[1,2,3,32,2048]{4,2,1,0,3:T(4,128)(2,1)S(1)}, u32[]{:S(2)}, u32[]{:S(2)}) async-start(bf16[1,2,3,32,2048]{4,2,1,0,3:T(4,128)(2,1)} %copy.7), calls=%async_computation | async-start | bytes 2097152 | tf_op jit(solution)/shard_map/all_to_all | solution.py:26
  15.1 0.0 all-reduce.2.cloned.1.call-start
  15.2 1.0 convolution_convert_fusion.1
  16.2 14.4 %all-to-all-done = bf16[1,2,3,32,2048]{4,2,1,0,3:T(4,128)(2,1)S(1)} async-done(((bf16[1,2,3,32,2048]{4,2,1,0,3:T(4,128)(2,1)}), bf16[1,2,3,32,2048]{4,2,1,0,3:T(4,128)(2,1)S(1)}, u32[]{:S(2)}, u32[]{:S(2)}) %all-to-all-start) | async-done | bytes 786464 | tf_op jit(solution)/shard_map/all_to_all | solution.py:26
  30.5 0.9 copy.18
  31.5 0.6 reshape.33
  32.1 0.0 copy-start.2
  32.1 2.7 convolution_convert_fusion
  34.7 0.0 all-reduce.2.cloned.1.call-update
  34.8 0.0 copy-start.3
  34.8 120.6 %all-reduce.2.cloned.1.call-done = bf16[64,24576]{1,0:T(8,128)(2,1)} async-done(((bf16[64,24576]{1,0:T(8,128)(2,1)}), bf16[64,24576]{1,0:T(8,128)(2,1)}) %all-reduce.2.cloned.1.call-update) | async-done | bytes 3145744 | tf_op jit(solution)/shard_map/psum | solution.py:34
  155.4 7.9 %reshape.34 = f32[64,3,4,2048]{3,2,1,0:T(4,128)} reshape(bf16[64,24576]{1,0:T(8,128)(2,1)} %all-reduce.2.cloned.1.call-done) | data formatting | bytes 9437184 | tf_op jit(solution)/shard_map/reshape | solution.py:35
  163.3 0.0 copy-done.2
  163.3 4.5 %slice.25 = bf16[64,3,1,2048]{3,2,1,0:T(2,128)(2,1)S(1)} slice(f32[64,3,4,2048]{3,2,1,0:T(4,128)} %reshape.34), slice={[0:64], [0:3], [3:4], [0:2048]} | slice | bytes 1572864 | tf_op jit(solution)/shard_map/slice | solution.py:46
  167.8 0.5 copy.20
  168.2 1.9 collective-permute-start
  170.2 0.0 copy-done.3
  170.2 0.1 dynamic_slice.14
  170.3 2.3 slice-done.2
  172.6 2.7 copy.19
  175.4 0.0 collective-permute-done
  175.4 0.2 convert_element_type.42
  175.5 0.0 slice-done
  175.5 0.0 slice-done.1
  175.6 5.9 %pad_maximum_fusion = (f32[64,3,4,2048]{3,0,2,1:T(8,128)}, f32[64,3,4,2048]{3,0,2,1:T(8,128)S(1)}) fusion(f32[64,3,3,2048]{3,0,2,1:T(8,128)S(1)} %copy.19, f32[64,3,1,2048]{3,0,2,1:T(8,128)S(1)} %convert_element_type.42, f32[64,3,4,2048]{3,2,1,0:T(4,128)S(1)} %bitcast.21, f32[4]{0:T(128)S(1)} %dynamic_slice.14), kind=kLoop, calls=%fused_computation.1 | loop fusion | flops 4718592 | bytes 25165840 | tf_op jit(solution)/shard_map/concatenate | solution.py:48
  181.5 2.8 copy-done
  184.3 0.1 slice.24
  184.4 1.3 collective-permute-start.1
  185.7 0.1 broadcast_bitcast_fusion
  185.8 0.1 dynamic_slice.12
  185.9 0.1 broadcast_bitcast_fusion.1
  186.0 0.1 mul.70
  186.1 0.1 mul.71
  186.2 5.1 %slice.20 = f32[64,3,3,2048]{3,0,2,1:T(8,128)} slice(f32[64,3,4,2048]{3,0,2,1:T(8,128)} %copy-done), slice={[0:64], [0:3], [1:4], [0:2048]} | slice | bytes 9437184 | tf_op jit(solution)/shard_map/slice | solution.py:53
  191.3 0.0 slice-done.3
  191.3 6.7 %copy.11 = f32[64,3,4,2048]{3,2,1,0:T(4,128)} copy(f32[64,3,4,2048]{3,0,2,1:T(8,128)S(1)} %bitcast.23) | data formatting | bytes 12582912 | tf_op jit(solution)/shard_map/concatenate | solution.py:48
  198.0 8.0 %concatenate.11 = f32[64,24576]{1,0:T(8,128)} reshape(f32[64,3,4,2048]{3,2,1,0:T(4,128)} %copy.11) | data formatting | bytes 12582912 | tf_op jit(solution)/shard_map/concatenate | solution.py:48
  206.0 0.0 collective-permute-done.1
  206.0 1.3 convert_element_type.43
  207.3 2.8 pad_maximum_fusion.1
  210.1 6.6 %copy.13 = f32[64,3,4,2048]{3,2,1,0:T(4,128)} copy(f32[64,3,4,2048]{3,0,2,1:T(8,128)S(1)} %pad_maximum_fusion.1) | data formatting | bytes 12582912 | tf_op jit(solution)/shard_map/concatenate | solution.py:53
  216.7 8.1 %concatenate.13 = f32[64,24576]{1,0:T(8,128)} reshape(f32[64,3,4,2048]{3,2,1,0:T(4,128)} %copy.13) | data formatting | bytes 12582912 | tf_op jit(solution)/shard_map/concatenate | solution.py:53
  224.8 6.4 %fusion.2 = f32[16,64]{1,0:T(8,128)S(1)} fusion(bf16[16,24576]{1,0:T(8,128)(2,1)} %copy-done.2, f32[64,24576]{1,0:T(8,128)} %concatenate.13, f32[64,24576]{1,0:T(8,128)} %concatenate.11, f32[24576]{0:T(1024)S(1)} %bitcast.26, f32[24576]{0:T(1024)S(1)} %bitcast.27, bf16[64,24576]{1,0:T(8,128)(2,1)S(1)} %copy-done.1), kind=kOutput, calls=%fused_computation.11 | convolution fusion | flops 62914560 | bytes 16715776 | tf_op jit(solution)/shard_map/dot_general | solution.py:59
  231.2 0.1 bitcast_multiply_fusion
  231.3 46.2 %psum.15 = f32[64,64]{1,0:T(8,128)S(1)} all-reduce(f32[64,64]{1,0:T(8,128)S(1)} %bitcast_multiply_fusion), channel_id=1, replica_groups=mesh['slab'=8,'field'=4] {'slab','field'}, use_global_device_ids=true, to_apply=%region_1.0 | all-reduce | flops 4096 | bytes 32768 | tf_op jit(solution)/shard_map/psum | solution.py:66
  277.5 0.8 convolution_multiply_fusion
  278.3 0.6 dynamic-slice_bitcast_fusion
  (15 shorter events, 0.0 us)
Async XLA Ops:
  10.0 20.6 %all-to-all-start = ((bf16[1,2,3,32,2048]{4,2,1,0,3:T(4,128)(2,1)}), bf16[1,2,3,32,2048]{4,2,1,0,3:T(4,128)(2,1)S(1)}, u32[]{:S(2)}, u32[]{:S(2)}) async-start(bf16[1,2,3,32,2048]{4,2,1,0,3:T(4,128)(2,1)} %copy.7), calls=%async_computation | async-start | bytes 2097152 | tf_op jit(solution)/shard_map/all_to_all | solution.py:26
  15.1 140.3 %all-reduce.2.cloned.1.call-start = ((), (), s32[]{:S(2)}) async-start(), calls=%async_computation.1 | async-start | bytes 6291456 | tf_op jit(solution)/shard_map/psum | solution.py:34
  32.1 131.2 %copy-start.2 = (bf16[16,24576]{1,0:T(8,128)(2,1)}, bf16[16,24576]{1,0:T(8,128)(2,1)S(1)}, u32[]{:S(2)}) copy-start(bf16[16,24576]{1,0:T(8,128)(2,1)S(1)} %reshape.33) | copy-start | bytes 2359300
  34.8 135.4 %copy-start.3 = (s32[32]{0:T(128)S(1)}, s32[32]{0:T(128)}, u32[]{:S(2)}) copy-start(s32[32]{0:T(128)} %param.7) | copy-start | bytes 388
  168.2 7.1 %collective-permute-start = (bf16[64,3,1,2048]{3,0,2,1:T(8,128)(2,1)S(1)}, bf16[64,3,1,2048]{3,0,2,1:T(8,128)(2,1)S(1)}, u32[]{:S(2)}, u32[]{:S(2)}) collective-permute-start(bf16[64,3,1,2048]{3,0,2,1:T(8,128)(2,1)S(1)} %copy.20), channel_id=1, source_target_pairs={{0,4},{1,5},{2,6},{3,7},{4,8},{5,9},{6,10},{7,11},{8,12},{9,13},{1... | collective-permute-start | bytes 2359304 | tf_op jit(solution)/shard_map/ppermute | solution.py:10
  170.3 2.3 slice-start.2
  170.3 5.3 %slice-start = ((s8[6291456]{0:T(1024)(128)(4,1)}), s8[4194304]{0:T(1024)(128)(4,1)S(1)}, s32[]{:S(2)}) async-start(s8[6291456]{0:T(1024)(128)(4,1)} %bitcast.20), calls=%async_computation.2 | async-start | bytes 8388608
  172.6 2.9 %slice-start.1 = ((s8[6291456]{0:T(1024)(128)(4,1)}), s8[2097152]{0:T(1024)(128)(4,1)S(1)}, s32[]{:S(2)}) async-start(s8[6291456]{0:T(1024)(128)(4,1)} %bitcast.20), calls=%async_computation.3 | async-start | bytes 4194304
  181.5 2.8 copy-start
  181.5 9.9 %slice-start.3 = ((s8[6291456]{0:T(1024)(128)(4,1)}), s8[2097152]{0:T(1024)(128)(4,1)S(1)}, s32[]{:S(2)}) async-start(s8[6291456]{0:T(1024)(128)(4,1)} %bitcast.22), calls=%async_computation.5 | async-start | bytes 4194304
  184.4 21.6 %collective-permute-start.1 = (bf16[64,3,1,2048]{3,0,2,1:T(8,128)(2,1)S(1)}, bf16[64,3,1,2048]{3,0,2,1:T(8,128)(2,1)}, u32[]{:S(2)}, u32[]{:S(2)}) collective-permute-start(bf16[64,3,1,2048]{3,0,2,1:T(8,128)(2,1)S(1)} %slice.24), channel_id=1, source_target_pairs={{4,0},{5,1},{6,2},{7,3},{8,4},{9,5},{10,6},{11,7},{12,8},{13,9},{1... | collective-permute-start | bytes 2359304 | tf_op jit(solution)/shard_map/ppermute | solution.py:10
  186.2 5.1 %slice-start.4 = ((s8[6291456]{0:T(1024)(128)(4,1)}), s8[4194304]{0:T(1024)(128)(4,1)S(1)}, s32[]{:S(2)}) async-start(s8[6291456]{0:T(1024)(128)(4,1)} %bitcast.22), calls=%async_computation.6 | async-start | bytes 8388608
  216.7 8.1 %copy-start.1 = (bf16[64,24576]{1,0:T(8,128)(2,1)S(1)}, bf16[64,24576]{1,0:T(8,128)(2,1)}, u32[]{:S(2)}) copy-start(bf16[64,24576]{1,0:T(8,128)(2,1)} %all-reduce.2.cloned.1.call-done) | copy-start | bytes 9437188
Sparse Core Ops, SparseCore 0:
  34.9 120.4 all-reduce.1
where the time goes:
time: 286 us
  waiting for transfers between devices  135 us (47%)
  local copies, waits for them, and re-layouts  60.8 us (21%)
  blocking collectives  46.2 us (16%)
  between operations  14.2 us (5%)
  matrix products  10.9 us (4%)
  other arithmetic  10.2 us (4%)
  starting transfers between devices  8.43 us (3%)
    psum x1, waiting for transfers between devices, body(): lax.psum(partial_z.astype(jnp.bfloat16), 'field').astype(jnp.float32)  121 us
    psum x1, blocking collectives, body(): rows = lax.psum(stored_rows, ('slab', 'field'))  46.2 us
    concatenate x2, local copies, waits for them, and re-layouts, body(): above = jnp.concatenate([flux[:, :, 1:], upper], axis=2)  14.7 us
    concatenate x2, local copies, waits for them, and re-layouts, body(): below = jnp.concatenate([lower, sketched[:, :, :-1]], axis=2)  14.6 us
    all_to_all x1, waiting for transfers between devices, body(): lax.all_to_all(snaps, 'slab', split_axis=3, concat_axis=1, tiled=True)  14.4 us
    unnamed x23, local copies, waits for them, and re-layouts  9.04 us
    reshape x1, local copies, waits for them, and re-layouts, body(): sketched = sketched.reshape(sketch_cols, comps, planes_dev, cells)  7.87 us
    dot_general x1, matrix products, body(): lax.dot_general(flat, applied, (((1,), (1,)), ((), ())), preferred_elemen...  6.4 us
  transfers between devices with their start and end apart: 4, of which 2 were waited for; matrix products, arithmetic and copies ran while one was open for 8% of the time, Pallas kernels for 0%

commit v1 on v0

--- a/solution.py
+++ b/solution.py
@@ -63,7 +63,7 @@
     stored_rows = (blocks[:, None, None] * partial_rows[None, :, :]).reshape(
         total_snaps, sketch_cols
     )
-    rows = lax.psum(stored_rows, ("slab", "field"))
+    rows = jnp.sum(lax.all_gather(stored_rows, ("slab", "field")), axis=0)
     core = (
         jnp.dot(test_all.astype(jnp.float32).T, rows, precision=lax.Precision.HIGHEST) / total_snaps
     )

time: 286 us -> 324 us (1.13)
  blocking collectives: 46.2 us -> 83.4 us
    all_gather x0 -> x1, blocking collectives: none -> 83.4 us  [body(): rows = jnp.sum(lax.all_gather(stored_rows, ('slab', 'field')), axis=0)]
    psum x1 -> x0, blocking collectives: 46.2 us -> none  [body(): rows = lax.psum(stored_rows, ('slab', 'field'))]
  transfers between devices with their start and end apart: 4 -> 4, of which waited for: 2 -> 2; matrix products, arithmetic and copies ran while one was open for 8% -> 7% of each run, Pallas kernels for 0% -> 0%
where the time goes in v1:
time: 324 us; the launch traced here: 323 us
  waiting for transfers between devices  135 us (42%)
  blocking collectives  83.4 us (26%)
  local copies, waits for them, and re-layouts  60.8 us (19%)
  between operations  14.2 us (4%)
  matrix products  10.9 us (3%)
  other arithmetic  10.3 us (3%)
  starting transfers between devices  8.43 us (3%)
    psum x1, waiting for transfers between devices, body(): lax.psum(partial_z.astype(jnp.bfloat16), 'field').astype(jnp.float32)  121 us
    all_gather x1, blocking collectives, body(): rows = jnp.sum(lax.all_gather(stored_rows, ('slab', 'field')), axis=0)  83.4 us
    concatenate x2, local copies, waits for them, and re-layouts, body(): above = jnp.concatenate([flux[:, :, 1:], upper], axis=2)  14.7 us
    concatenate x2, local copies, waits for them, and re-layouts, body(): below = jnp.concatenate([lower, sketched[:, :, :-1]], axis=2)  14.6 us
    all_to_all x1, waiting for transfers between devices, body(): lax.all_to_all(snaps, 'slab', split_axis=3, concat_axis=1, tiled=True)  14.4 us
    unnamed x23, local copies, waits for them, and re-layouts  9.04 us
    reshape x1, local copies, waits for them, and re-layouts, body(): sketched = sketched.reshape(sketch_cols, comps, planes_dev, cells)  7.87 us
  transfers between devices with their start and end apart: 4, of which 2 were waited for; matrix products, arithmetic and copies ran while one was open for 7% of the time, Pallas kernels for 0%

profile of v1, /device:TPU:0, one launch (start us, length us, event | category | flops | bytes accessed | tf_op | source)
XLA Modules:
  0.0 323.0 jit_solution(4980729886656057329)
XLA Ops:
  7.2 2.8 copy.7
  10.0 5.2 %all-to-all-start = ((bf16[1,2,3,32,2048]{4,2,1,0,3:T(4,128)(2,1)}), bf16[1,2,3,32,2048]{4,2,1,0,3:T(4,128)(2,1)S(1)}, u32[]{:S(2)}, u32[]{:S(2)}) async-start(bf16[1,2,3,32,2048]{4,2,1,0,3:T(4,128)(2,1)} %copy.7), calls=%async_computation | async-start | bytes 2097152 | tf_op jit(solution)/shard_map/all_to_all | solution.py:26
  15.1 0.0 all-reduce.2.cloned.1.call-start
  15.2 1.0 convolution_convert_fusion.1
  16.2 14.4 %all-to-all-done = bf16[1,2,3,32,2048]{4,2,1,0,3:T(4,128)(2,1)S(1)} async-done(((bf16[1,2,3,32,2048]{4,2,1,0,3:T(4,128)(2,1)}), bf16[1,2,3,32,2048]{4,2,1,0,3:T(4,128)(2,1)S(1)}, u32[]{:S(2)}, u32[]{:S(2)}) %all-to-all-start) | async-done | bytes 786464 | tf_op jit(solution)/shard_map/all_to_all | solution.py:26
  30.5 0.9 copy.18
  31.5 0.6 reshape.64
  32.1 0.0 copy-start.2
  32.1 2.7 convolution_convert_fusion
  34.7 0.0 all-reduce.2.cloned.1.call-update
  34.8 0.0 copy-start.3
  34.8 120.6 %all-reduce.2.cloned.1.call-done = bf16[64,24576]{1,0:T(8,128)(2,1)} async-done(((bf16[64,24576]{1,0:T(8,128)(2,1)}), bf16[64,24576]{1,0:T(8,128)(2,1)}) %all-reduce.2.cloned.1.call-update) | async-done | bytes 3145744 | tf_op jit(solution)/shard_map/psum | solution.py:34
  155.4 7.9 %reshape.65 = f32[64,3,4,2048]{3,2,1,0:T(4,128)} reshape(bf16[64,24576]{1,0:T(8,128)(2,1)} %all-reduce.2.cloned.1.call-done) | data formatting | bytes 9437184 | tf_op jit(solution)/shard_map/reshape | solution.py:35
  163.3 0.0 copy-done.2
  163.3 4.5 %slice.25 = bf16[64,3,1,2048]{3,2,1,0:T(2,128)(2,1)S(1)} slice(f32[64,3,4,2048]{3,2,1,0:T(4,128)} %reshape.65), slice={[0:64], [0:3], [3:4], [0:2048]} | slice | bytes 1572864 | tf_op jit(solution)/shard_map/slice | solution.py:46
  167.8 0.5 copy.20
  168.2 1.9 collective-permute-start
  170.2 0.0 copy-done.3
  170.2 0.1 dynamic_slice.14
  170.3 2.3 slice-done.2
  172.6 2.7 copy.19
  175.4 0.0 collective-permute-done
  175.4 0.2 convert_element_type.42
  175.5 0.0 slice-done
  175.6 5.9 %pad_maximum_fusion = (f32[64,3,4,2048]{3,0,2,1:T(8,128)}, f32[64,3,4,2048]{3,0,2,1:T(8,128)S(1)}) fusion(f32[64,3,3,2048]{3,0,2,1:T(8,128)S(1)} %copy.19, f32[64,3,1,2048]{3,0,2,1:T(8,128)S(1)} %convert_element_type.42, f32[64,3,4,2048]{3,2,1,0:T(4,128)S(1)} %bitcast.22, f32[4]{0:T(128)S(1)} %dynamic_slice.14), kind=kLoop, calls=%fused_computation.1 | loop fusion | flops 4718592 | bytes 25165840 | tf_op jit(solution)/shard_map/concatenate | solution.py:48
  181.5 2.8 copy-done
  184.3 0.1 slice.24
  184.4 1.3 collective-permute-start.1
  185.7 0.1 broadcast_bitcast_fusion
  185.8 0.1 dynamic_slice.12
  185.9 0.1 broadcast_bitcast_fusion.1
  186.0 0.1 mul.76
  186.1 0.1 mul.77
  186.2 5.1 %slice.20 = f32[64,3,3,2048]{3,0,2,1:T(8,128)} slice(f32[64,3,4,2048]{3,0,2,1:T(8,128)} %copy-done), slice={[0:64], [0:3], [1:4], [0:2048]} | slice | bytes 9437184 | tf_op jit(solution)/shard_map/slice | solution.py:53
  191.3 0.0 slice-done.3
  191.3 6.7 %copy.11 = f32[64,3,4,2048]{3,2,1,0:T(4,128)} copy(f32[64,3,4,2048]{3,0,2,1:T(8,128)S(1)} %bitcast.24) | data formatting | bytes 12582912 | tf_op jit(solution)/shard_map/concatenate | solution.py:48
  198.0 8.0 %concatenate.11 = f32[64,24576]{1,0:T(8,128)} reshape(f32[64,3,4,2048]{3,2,1,0:T(4,128)} %copy.11) | data formatting | bytes 12582912 | tf_op jit(solution)/shard_map/concatenate | solution.py:48
  206.0 0.0 collective-permute-done.1
  206.0 1.3 convert_element_type.43
  207.3 2.8 pad_maximum_fusion.1
  210.1 6.6 %copy.13 = f32[64,3,4,2048]{3,2,1,0:T(4,128)} copy(f32[64,3,4,2048]{3,0,2,1:T(8,128)S(1)} %pad_maximum_fusion.1) | data formatting | bytes 12582912 | tf_op jit(solution)/shard_map/concatenate | solution.py:53
  216.7 8.1 %concatenate.13 = f32[64,24576]{1,0:T(8,128)} reshape(f32[64,3,4,2048]{3,2,1,0:T(4,128)} %copy.13) | data formatting | bytes 12582912 | tf_op jit(solution)/shard_map/concatenate | solution.py:53
  224.8 6.4 %fusion.2 = f32[16,64]{1,0:T(8,128)S(1)} fusion(bf16[16,24576]{1,0:T(8,128)(2,1)} %copy-done.2, f32[64,24576]{1,0:T(8,128)} %concatenate.13, f32[64,24576]{1,0:T(8,128)} %concatenate.11, f32[24576]{0:T(1024)S(1)} %bitcast.27, f32[24576]{0:T(1024)S(1)} %bitcast.28, bf16[64,24576]{1,0:T(8,128)(2,1)S(1)} %copy-done.1), kind=kOutput, calls=%fused_computation.11 | convolution fusion | flops 62914560 | bytes 16715776 | tf_op jit(solution)/shard_map/dot_general | solution.py:59
  231.2 0.1 bitcast_multiply_fusion
  231.3 83.4 %all_gather.3 = f32[32,64,64]{2,1,0:T(8,128)S(1)} all-gather(f32[1,64,64]{2,1,0:T(8,128)S(1)} %bitcast_multiply_fusion), channel_id=1, replica_groups=mesh['slab'=8,'field'=4] {'slab','field'}, dimensions={0}, use_global_device_ids=true | all-gather | bytes 540672 | tf_op jit(solution)/shard_map/all_gather | solution.py:66
  314.7 0.1 reduce_sum.9
  314.8 0.8 convolution_multiply_fusion
  315.6 0.6 dynamic-slice_bitcast_fusion
  (17 shorter events, 0.1 us)
Async XLA Ops:
  10.0 20.6 %all-to-all-start = ((bf16[1,2,3,32,2048]{4,2,1,0,3:T(4,128)(2,1)}), bf16[1,2,3,32,2048]{4,2,1,0,3:T(4,128)(2,1)S(1)}, u32[]{:S(2)}, u32[]{:S(2)}) async-start(bf16[1,2,3,32,2048]{4,2,1,0,3:T(4,128)(2,1)} %copy.7), calls=%async_computation | async-start | bytes 2097152 | tf_op jit(solution)/shard_map/all_to_all | solution.py:26
  15.1 140.3 %all-reduce.2.cloned.1.call-start = ((), (), s32[]{:S(2)}) async-start(), calls=%async_computation.1 | async-start | bytes 6291456 | tf_op jit(solution)/shard_map/psum | solution.py:34
  32.1 131.2 %copy-start.2 = (bf16[16,24576]{1,0:T(8,128)(2,1)}, bf16[16,24576]{1,0:T(8,128)(2,1)S(1)}, u32[]{:S(2)}) copy-start(bf16[16,24576]{1,0:T(8,128)(2,1)S(1)} %reshape.64) | copy-start | bytes 2359300
  34.8 135.4 %copy-start.3 = (s32[32]{0:T(128)S(1)}, s32[32]{0:T(128)}, u32[]{:S(2)}) copy-start(s32[32]{0:T(128)} %param.7) | copy-start | bytes 388
  168.2 7.1 %collective-permute-start = (bf16[64,3,1,2048]{3,0,2,1:T(8,128)(2,1)S(1)}, bf16[64,3,1,2048]{3,0,2,1:T(8,128)(2,1)S(1)}, u32[]{:S(2)}, u32[]{:S(2)}) collective-permute-start(bf16[64,3,1,2048]{3,0,2,1:T(8,128)(2,1)S(1)} %copy.20), channel_id=1, source_target_pairs={{0,4},{1,5},{2,6},{3,7},{4,8},{5,9},{6,10},{7,11},{8,12},{9,13},{1... | collective-permute-start | bytes 2359304 | tf_op jit(solution)/shard_map/ppermute | solution.py:10
  170.3 2.3 slice-start.2
  170.3 5.3 %slice-start = ((s8[6291456]{0:T(1024)(128)(4,1)}), s8[4194304]{0:T(1024)(128)(4,1)S(1)}, s32[]{:S(2)}) async-start(s8[6291456]{0:T(1024)(128)(4,1)} %bitcast.21), calls=%async_computation.2 | async-start | bytes 8388608
  172.6 2.9 slice-start.1
  181.5 2.8 copy-start
  181.5 9.9 %slice-start.3 = ((s8[6291456]{0:T(1024)(128)(4,1)}), s8[2097152]{0:T(1024)(128)(4,1)S(1)}, s32[]{:S(2)}) async-start(s8[6291456]{0:T(1024)(128)(4,1)} %bitcast.23), calls=%async_computation.5 | async-start | bytes 4194304
  184.4 21.6 %collective-permute-start.1 = (bf16[64,3,1,2048]{3,0,2,1:T(8,128)(2,1)S(1)}, bf16[64,3,1,2048]{3,0,2,1:T(8,128)(2,1)}, u32[]{:S(2)}, u32[]{:S(2)}) collective-permute-start(bf16[64,3,1,2048]{3,0,2,1:T(8,128)(2,1)S(1)} %slice.24), channel_id=1, source_target_pairs={{4,0},{5,1},{6,2},{7,3},{8,4},{9,5},{10,6},{11,7},{12,8},{13,9},{1... | collective-permute-start | bytes 2359304 | tf_op jit(solution)/shard_map/ppermute | solution.py:10
  186.2 5.1 %slice-start.4 = ((s8[6291456]{0:T(1024)(128)(4,1)}), s8[4194304]{0:T(1024)(128)(4,1)S(1)}, s32[]{:S(2)}) async-start(s8[6291456]{0:T(1024)(128)(4,1)} %bitcast.23), calls=%async_computation.6 | async-start | bytes 8388608
  216.7 8.1 %copy-start.1 = (bf16[64,24576]{1,0:T(8,128)(2,1)S(1)}, bf16[64,24576]{1,0:T(8,128)(2,1)}, u32[]{:S(2)}) copy-start(bf16[64,24576]{1,0:T(8,128)(2,1)} %all-reduce.2.cloned.1.call-done) | copy-start | bytes 9437188
Sparse Core Ops, SparseCore 0:
  34.9 120.4 all-reduce.1
